TPU v7x, 32 devices: a whole 2x2x4 slice. The times are simulated.
32 devices in a mesh: group: 16 (over z, y, x), depth: 2 (over core).
Axes of the slice: x: 2, y: 2, z: 4, core: 2. Of those that a mesh axis runs over, the one named last changes fastest.
Arguments:
- fwd_now: float32 [125, 8192], P(None, ('group', 'depth')), may hold values from -6 to 6
- fwd_prev: float32 [125, 8192], P(None, ('group', 'depth')), may hold values from -6 to 6
- adj_now: float32 [125, 8192], P(None, ('group', 'depth')), may hold values from -6 to 6
- adj_prev: float32 [125, 8192], P(None, ('group', 'depth')), may hold values from -6 to 6
- speed_sq: float32 [8192], P(('group', 'depth')), may hold values from 0.5 to 2
- face_lists: int32 [6, 8192], P(None, ('group', 'depth')), may hold values from 0 to 511, as said below
- send_low: int32 [8192], P(('group', 'depth')), may hold values from 0 to 255, as said below
- send_high: int32 [8192], P(('group', 'depth')), may hold values from 0 to 255, as said below
- send_radial: int32 [512], P(('group', 'depth')), may hold values from 0 to 255, as said below
- owner_dev: int32 [8192, 1], P(('group', 'depth')), may hold values from 0 to 31; in each aligned block of 256 rows (0 to 255, 256 to 511, ...) at most 14 rows name the same one
- param_slot: int32 [8192], P(('group', 'depth')), may hold values from 0 to 127
Outputs:
- fwd_out: float32 [125, 8192], P(None, ('group', 'depth'))
- adj_out: float32 [125, 8192], P(None, ('group', 'depth'))
- param_grad: float32 [4096, 125], P(('group', 'depth'))
Inputs may be any that keep to these rules, and one draw needn't show every extreme that they name: Each device's elements form a structured block of 1 x 16 x 16 elements stored in a device-specific order; face_lists names each element's touching face in its direction's pool, or the pool's last zero entry at an outer surface or a side of the block along the second lateral direction. `send_low`: distinct elements of one device, ordered by position on the face. `send_high`: distinct elements of one device, ordered by position on the face. `send_radial`: distinct elements of one device: the top layer on depth 0, the bottom layer on depth 1. `owner_dev`: among the elements of one device, no owner is named more than 14 times.
All inputs are finite; a program needn't handle non-finite values.
Results may differ from a plain program's by a relative error of at most 0.0001.
Values sent between devices are 32-bit elements; how exact they have to be, the bound alone decides.
A program may use at most 64 MiB of HBM per device.

v0:
```python
import math

import jax
import jax.numpy as jnp
import numpy as np
from jax import lax
from jax.sharding import PartitionSpec as P

NODES = 125
STEPS = 4
P_DEV = 128


PENALTY = 40.0
DT_SQUARED = 0.001
KERNEL_SCALE = 0.05
HIGH = lax.Precision.HIGHEST


def from_behind(block, axis, distance):
    devices = range(lax.axis_size(axis))
    route = [((i - distance) % len(devices), i) for i in devices]
    return lax.ppermute(block, axis, route)


def swapped(block, axis, apart):
    count = lax.axis_size(axis)
    route = []
    for low in range(count):
        high = low | 1 << apart
        if high != low and high < count:
            route += [(low, high), (high, low)]
    return lax.ppermute(block, axis, route)


def gll_tables():
    points = np.array([-1.0, -math.sqrt(3.0 / 7.0), 0.0, math.sqrt(3.0 / 7.0), 1.0])
    weights = np.array([0.1, 49.0 / 90.0, 32.0 / 45.0, 49.0 / 90.0, 0.1])
    barycentric = np.array(
        [np.prod([points[i] - points[m] for m in range(5) if m != i]) for i in range(5)]
    )
    derivative = np.zeros((5, 5))
    for i in range(5):
        for j in range(5):
            if i != j:
                derivative[i, j] = barycentric[i] / (barycentric[j] * (points[i] - points[j]))
            else:
                derivative[i, j] = sum((1.0 / (points[i] - points[m]) for m in range(5) if m != i))
    return (weights, derivative)


def node_tables():
    weights, derivative = gll_tables()
    single = np.eye(5)
    operators = [
        np.kron(derivative, np.kron(single, single)),
        np.kron(single, np.kron(derivative, single)),
        np.kron(single, np.kron(single, derivative)),
    ]
    cube = np.kron(weights, np.kron(weights, weights))
    digits = [(n // 25, n // 5 % 5, n % 5) for n in range(125)]
    rows = []
    for f in range(6):
        axis_pick = f // 2
        level = 0 if f % 2 == 0 else 4
        rows.append([n for n in range(125) if digits[n][axis_pick] == level])
    square = np.kron(weights, weights)
    spread = np.zeros((125, 150))
    for f in range(6):
        for a, n in enumerate(rows[f]):
            spread[n, 25 * f + a] = 1.0
    return (operators, cube, rows, square, spread)


def apply_nodes(matrix, field):
    return jnp.einsum("mn,n...->m...", jnp.asarray(matrix, jnp.float32), field, precision=HIGH)


def per_device(
    fwd_now,
    fwd_prev,
    adj_now,
    adj_prev,
    speed_sq,
    face_lists,
    send_low,
    send_high,
    send_radial,
    owner_dev,
    param_slot,
):
    operators, cube_np, rows, square_np, spread_np = node_tables()
    elements = fwd_now.shape[1]
    groups = lax.axis_size("group")
    layers = lax.axis_size("depth")
    devices = groups * layers
    capacity = elements // devices + elements // (2 * devices) + 2
    state = jnp.stack([fwd_now, adj_now], axis=1)
    previous = jnp.stack([fwd_prev, adj_prev], axis=1)
    depth_here = lax.axis_index("depth")
    cube = jnp.asarray(cube_np, jnp.float32).reshape(125, 1, 1)
    square = jnp.asarray(square_np, jnp.float32).reshape(25, 1, 1)
    row_ids = [jnp.asarray(np.array(r), jnp.int32) for r in rows]
    target = owner_dev[:, 0]
    onehot = (target[:, None] == jnp.arange(devices, dtype=jnp.int32)[None, :]).astype(jnp.int32)
    before = jnp.cumsum(onehot, axis=0) - onehot
    position = jnp.sum(before * onehot, axis=1)
    placing = target * capacity + position
    placer = (jnp.arange(devices * capacity, dtype=jnp.int32)[:, None] == placing[None, :]).astype(
        jnp.float32
    )
    labels = (
        jnp.dot(
            placer,
            param_slot.astype(jnp.float32) + 1.0,
            precision=HIGH,
            preferred_element_type=jnp.float32,
        )
        - 1.0
    )
    labels = labels.reshape(groups, layers, capacity)
    cell_ids = jnp.arange(P_DEV, dtype=jnp.float32)[:, None]
    param_grad = jnp.zeros((P_DEV, NODES), jnp.float32)
    for step in range(STEPS):
        grads = [apply_nodes(operators[d], state) for d in range(3)]
        product = (
            grads[0][:, 0] * grads[0][:, 1]
            + grads[1][:, 0] * grads[1][:, 1]
            + grads[2][:, 0] * grads[2][:, 1]
        )
        kernel = KERNEL_SCALE * cube[:, 0] * speed_sq * product
        blocks = lax.dot_general(
            placer,
            kernel,
            (((1,), (1,)), ((), ())),
            precision=HIGH,
            preferred_element_type=jnp.float32,
        )
        got_blocks = lax.all_to_all(
            lax.all_to_all(
                blocks.reshape(groups, layers, capacity, NODES),
                "group",
                split_axis=0,
                concat_axis=0,
                tiled=True,
            ),
            "depth",
            split_axis=1,
            concat_axis=1,
            tiled=True,
        )
        got_labels = lax.all_to_all(
            lax.all_to_all(labels, "group", split_axis=0, concat_axis=0, tiled=True),
            "depth",
            split_axis=1,
            concat_axis=1,
            tiled=True,
        )
        selector = (got_labels.reshape(1, -1) == cell_ids).astype(jnp.float32)
        param_grad = param_grad + jnp.dot(
            selector,
            got_blocks.reshape(-1, NODES),
            precision=HIGH,
            preferred_element_type=jnp.float32,
        )
        faces = [jnp.take(state, row_ids[f], axis=0) for f in range(6)]
        from_low = from_behind(faces[1][..., send_high], "group", 1)
        from_high = from_behind(faces[0][..., send_low], "group", -1)
        sent_radial = jnp.where(
            depth_here == 0, faces[5][..., send_radial], faces[4][..., send_radial]
        )
        from_radial = swapped(sent_radial, "depth", 0)
        halos = [from_low, from_high, None, None, from_radial, from_radial]
        zero_face = jnp.zeros((25, 2, 1), jnp.float32)
        jumps = []
        for f in range(6):
            members = [faces[f ^ 1]] + ([halos[f]] if halos[f] is not None else []) + [zero_face]
            pool = jnp.concatenate(members, axis=-1)
            picker = (
                jnp.arange(pool.shape[-1], dtype=jnp.int32)[:, None] == face_lists[f][None, :]
            ).astype(jnp.float32)
            other = jnp.einsum("afm,me->afe", pool, picker, precision=HIGH)
            jumps.append(PENALTY * square * (faces[f] - other))
        penal = apply_nodes(spread_np, jnp.concatenate(jumps, axis=0))
        stiff = apply_nodes(operators[0].T, cube * speed_sq * grads[0])
        stiff = stiff + apply_nodes(operators[1].T, cube * speed_sq * grads[1])
        stiff = stiff + apply_nodes(operators[2].T, cube * speed_sq * grads[2])
        accel = -(stiff + penal) / cube
        following = 2.0 * state - previous + DT_SQUARED * accel
        previous = state
        state = following
    return (state[:, 0], state[:, 1], param_grad)


def solution(mesh):
    return jax.shard_map(
        per_device,
        mesh=mesh,
        in_specs=(
            P(None, ("group", "depth")),
            P(None, ("group", "depth")),
            P(None, ("group", "depth")),
            P(None, ("group", "depth")),
            P(("group", "depth")),
            P(None, ("group", "depth")),
            P(("group", "depth")),
            P(("group", "depth")),
            P(("group", "depth")),
            P(("group", "depth"), None),
            P(("group", "depth")),
        ),
        out_specs=(
            P(None, ("group", "depth")),
            P(None, ("group", "depth")),
            P(("group", "depth"), None),
        ),
        check_vma=False,
    )
```

profile of v0, /device:TPU:0, one launch (start us, length us, event | category | flops | bytes accessed | tf_op | source)
XLA Modules:
  0.0 178.7 jit_solution(6949498502727132853)
XLA Ops:
  0.7 0.7 convert_add_fusion
  1.4 0.7 fusion.236
  2.9 0.8 fusion.235
  3.7 0.7 multiply_add_fusion.1
  4.6 0.8 reshape.216
  5.4 8.3 %all-to-all-start = ((f32[16,2,14]{2,1,0:T(2,128)}), f32[16,2,14]{2,1,0:T(2,128)S(1)}, u32[]{:S(2)}, u32[]{:S(2)}) async-start(f32[16,2,14]{2,1,0:T(2,128)} %reshape.216), calls=%async_computation | async-start | bytes 32768 | tf_op jit(solution)/shard_map/all_to_all | solution.py:153
  14.9 1.0 gather_fusion.1
  16.0 5.6 %collective-permute-start.1 = (f32[25,2,256]{2,0,1:T(8,128)S(1)}, f32[25,2,256]{2,0,1:T(8,128)S(1)}, u32[]{:S(2)}, u32[]{:S(2)}) collective-permute-start(f32[25,2,256]{2,0,1:T(8,128)S(1)} %bitcast.204), channel_id=1, source_target_pairs={{2,0},{4,2},{6,4},{8,6},{10,8},{12,10},{14,12},{16,14},{18,16},{20... | collective-permute-start | bytes 153608 | tf_op jit(solution)/shard_map/ppermute | solution.py:23
  22.4 1.0 gather_fusion
  24.3 0.6 gather_fusion.20
  33.8 0.9 copy.461
  35.3 3.7 %all_to_all.56 = f32[2,1,224]{2,1,0:T(1,128)S(1)} all-to-all(f32[2,1,224]{2,1,0:T(1,128)S(1)} %reshape.633), channel_id=1, replica_groups=mesh['group'=16,'depth'=2] {'depth'}, dimensions={0} | all-to-all | bytes 3584 | tf_op jit(solution)/shard_map/all_to_all | solution.py:152
  39.0 7.0 %all-to-all-start.2 = ((f32[16,2,14,125]{3,1,2,0:T(2,128)}), f32[16,2,14,125]{3,1,2,0:T(2,128)S(1)}, u32[]{:S(2)}, u32[]{:S(2)}) async-start(f32[16,2,14,125]{3,1,2,0:T(2,128)} %copy.461), calls=%async_computation.2 | async-start | bytes 458752 | tf_op jit(solution)/shard_map/all_to_all | solution.py:140
  46.5 0.7 reduce.2
  48.1 0.7 concatenate.90
  59.0 0.9 copy.464
  60.1 1.0 gather_fusion.5
  61.2 5.6 %collective-permute-start.4 = (f32[25,2,256]{2,0,1:T(8,128)S(1)}, f32[25,2,256]{2,0,1:T(8,128)S(1)}, u32[]{:S(2)}, u32[]{:S(2)}) collective-permute-start(f32[25,2,256]{2,0,1:T(8,128)S(1)} %bitcast.207), channel_id=1, source_target_pairs={{2,0},{4,2},{6,4},{8,6},{10,8},{12,10},{14,12},{16,14},{18,16},{20... | collective-permute-start | bytes 153608 | tf_op jit(solution)/shard_map/ppermute | solution.py:23
  66.7 1.0 gather_fusion.4
  69.1 6.9 %collective-permute-done.3 = f32[25,2,256]{2,0,1:T(8,128)S(1)} collective-permute-done((f32[25,2,256]{2,0,1:T(8,128)S(1)}, f32[25,2,256]{2,0,1:T(8,128)S(1)}, u32[]{:S(2)}, u32[]{:S(2)}) %collective-permute-start.3) | collective-permute-done | bytes 51232 | tf_op jit(solution)/shard_map/ppermute | solution.py:23
  76.3 0.7 concatenate.97
  78.4 0.6 gather_fusion.32
  86.9 0.9 copy.467
  88.0 1.0 gather_fusion.9
  89.1 1.0 gather_fusion.8
  90.2 2.3 %collective-permute-start.6 = (f32[25,2,256]{2,0,1:T(8,128)S(1)}, f32[25,2,256]{2,0,1:T(8,128)S(1)}, u32[]{:S(2)}, u32[]{:S(2)}) collective-permute-start(f32[25,2,256]{2,0,1:T(8,128)S(1)} %bitcast.210), channel_id=1, source_target_pairs={{30,0},{0,2},{2,4},{4,6},{6,8},{8,10},{10,12},{12,14},{14,16},{16,... | collective-permute-start | bytes 153608 | tf_op jit(solution)/shard_map/ppermute | solution.py:23
  93.9 4.7 %collective-permute-done.6 = f32[25,2,256]{2,0,1:T(8,128)S(1)} collective-permute-done((f32[25,2,256]{2,0,1:T(8,128)S(1)}, f32[25,2,256]{2,0,1:T(8,128)S(1)}, u32[]{:S(2)}, u32[]{:S(2)}) %collective-permute-start.6) | collective-permute-done | bytes 51232 | tf_op jit(solution)/shard_map/ppermute | solution.py:23
  99.0 0.7 concatenate.104
  109.6 0.9 copy.470
  110.6 1.0 gather_fusion.13
  111.8 1.0 gather_fusion.12
  112.9 2.1 %collective-permute-start.9 = (f32[25,2,256]{2,0,1:T(8,128)S(1)}, f32[25,2,256]{2,0,1:T(8,128)S(1)}, u32[]{:S(2)}, u32[]{:S(2)}) collective-permute-start(f32[25,2,256]{2,0,1:T(8,128)S(1)} %bitcast.211), channel_id=1, source_target_pairs={{30,0},{0,2},{2,4},{4,6},{6,8},{8,10},{10,12},{12,14},{14,16},{16,... | collective-permute-start | bytes 153608 | tf_op jit(solution)/shard_map/ppermute | solution.py:23
  115.5 5.5 %collective-permute-done.9 = f32[25,2,256]{2,0,1:T(8,128)S(1)} collective-permute-done((f32[25,2,256]{2,0,1:T(8,128)S(1)}, f32[25,2,256]{2,0,1:T(8,128)S(1)}, u32[]{:S(2)}, u32[]{:S(2)}) %collective-permute-start.9) | collective-permute-done | bytes 51232 | tf_op jit(solution)/shard_map/ppermute | solution.py:23
  121.4 3.5 %all-to-all-start.4 = ((f32[16,2,14,125]{3,1,2,0:T(2,128)}), f32[16,2,14,125]{3,1,2,0:T(2,128)S(1)}, u32[]{:S(2)}, u32[]{:S(2)}) async-start(f32[16,2,14,125]{3,1,2,0:T(2,128)} %copy.464), calls=%async_computation.4 | async-start | bytes 458752 | tf_op jit(solution)/shard_map/all_to_all | solution.py:140
  125.3 0.7 concatenate.111
  126.6 0.7 copy.462
  127.3 7.0 %all-to-all-done.4 = f32[16,2,14,125]{3,1,2,0:T(2,128)S(1)} async-done(((f32[16,2,14,125]{3,1,2,0:T(2,128)}), f32[16,2,14,125]{3,1,2,0:T(2,128)S(1)}, u32[]{:S(2)}, u32[]{:S(2)}) %all-to-all-start.4) | async-done | bytes 224032 | tf_op jit(solution)/shard_map/all_to_all | solution.py:140
  134.3 3.4 %all-to-all-start.3 = ((f32[16,2,14,125]{3,0,2,1:T(8,128)}), f32[16,2,14,125]{3,0,2,1:T(8,128)S(1)}, u32[]{:S(2)}, u32[]{:S(2)}) async-start(f32[16,2,14,125]{3,0,2,1:T(8,128)} %copy.462), calls=%async_computation.3 | async-start | bytes 458752 | tf_op jit(solution)/shard_map/all_to_all | solution.py:139
  137.8 1.5 all-to-all-done.3
  139.3 3.9 %all_to_all.57 = f32[16,2,14,125]{3,0,2,1:T(8,128)S(1)} all-to-all(f32[16,2,14,125]{3,0,2,1:T(8,128)S(1)} %copy.465), channel_id=1, replica_groups=mesh['group'=16,'depth'=2] {'depth'}, dimensions={1} | all-to-all | bytes 448000 | tf_op jit(solution)/shard_map/all_to_all | solution.py:139
  143.2 3.5 %all-to-all-start.6 = ((f32[16,2,14,125]{3,1,2,0:T(2,128)}), f32[16,2,14,125]{3,1,2,0:T(2,128)S(1)}, u32[]{:S(2)}, u32[]{:S(2)}) async-start(f32[16,2,14,125]{3,1,2,0:T(2,128)} %copy.467), calls=%async_computation.6 | async-start | bytes 458752 | tf_op jit(solution)/shard_map/all_to_all | solution.py:140
  146.7 0.7 slice_bitcast_fusion
  147.9 8.6 %all-to-all-done.6 = f32[16,2,14,125]{3,1,2,0:T(2,128)S(1)} async-done(((f32[16,2,14,125]{3,1,2,0:T(2,128)}), f32[16,2,14,125]{3,1,2,0:T(2,128)S(1)}, u32[]{:S(2)}, u32[]{:S(2)}) %all-to-all-start.6) | async-done | bytes 224032 | tf_op jit(solution)/shard_map/all_to_all | solution.py:140
  156.5 3.9 %all_to_all.58 = f32[16,2,14,125]{3,0,2,1:T(8,128)S(1)} all-to-all(f32[16,2,14,125]{3,0,2,1:T(8,128)S(1)} %copy.468), channel_id=1, replica_groups=mesh['group'=16,'depth'=2] {'depth'}, dimensions={1} | all-to-all | bytes 448000 | tf_op jit(solution)/shard_map/all_to_all | solution.py:139
  160.4 3.5 %all-to-all-start.8 = ((f32[16,2,14,125]{3,1,2,0:T(2,128)}), f32[16,2,14,125]{3,1,2,0:T(2,128)S(1)}, u32[]{:S(2)}, u32[]{:S(2)}) async-start(f32[16,2,14,125]{3,1,2,0:T(2,128)} %copy.470), calls=%async_computation.8 | async-start | bytes 458752 | tf_op jit(solution)/shard_map/all_to_all | solution.py:140
  164.6 9.1 %all-to-all-done.8 = f32[16,2,14,125]{3,1,2,0:T(2,128)S(1)} async-done(((f32[16,2,14,125]{3,1,2,0:T(2,128)}), f32[16,2,14,125]{3,1,2,0:T(2,128)S(1)}, u32[]{:S(2)}, u32[]{:S(2)}) %all-to-all-start.8) | async-done | bytes 224032 | tf_op jit(solution)/shard_map/all_to_all | solution.py:140
  173.7 3.9 %all_to_all.59 = f32[16,2,14,125]{3,0,2,1:T(8,128)S(1)} all-to-all(f32[16,2,14,125]{3,0,2,1:T(8,128)S(1)} %copy.471), channel_id=1, replica_groups=mesh['group'=16,'depth'=2] {'depth'}, dimensions={1} | all-to-all | bytes 448000 | tf_op jit(solution)/shard_map/all_to_all | solution.py:139
  177.8 0.9 convolution_add_fusion.12
  (264 shorter events, 51.0 us)
Async XLA Ops:
  0.6 13.1 %copy-start.15 = (s32[256]{0:T(256)S(1)}, s32[256]{0:T(256)}, u32[]{:S(2)}) copy-start(s32[256]{0:T(256)} %param.55) | copy-start | bytes 3076
  0.6 13.1 %copy-start = (f32[125,256]{1,0:T(8,128)S(1)}, f32[125,256]{1,0:T(8,128)}, u32[]{:S(2)}) copy-start(f32[125,256]{1,0:T(8,128)} %param.51) | copy-start | bytes 384004
  0.7 13.1 %copy-start.1 = (f32[125,256]{1,0:T(8,128)S(1)}, f32[125,256]{1,0:T(8,128)}, u32[]{:S(2)}) copy-start(f32[125,256]{1,0:T(8,128)} %param.49) | copy-start | bytes 384004
  5.4 29.8 %all-to-all-start = ((f32[16,2,14]{2,1,0:T(2,128)}), f32[16,2,14]{2,1,0:T(2,128)S(1)}, u32[]{:S(2)}, u32[]{:S(2)}) async-start(f32[16,2,14]{2,1,0:T(2,128)} %reshape.216), calls=%async_computation | async-start | bytes 32768 | tf_op jit(solution)/shard_map/all_to_all | solution.py:153
  14.7 6.9 %copy-start.16 = (s32[256]{0:T(256)S(1)}, s32[256]{0:T(256)}, u32[]{:S(2)}) copy-start(s32[256]{0:T(256)} %param.56) | copy-start | bytes 3076
  14.7 6.9 %copy-start.21 = (s32[25]{0:T(128)S(1)}, s32[25]{0:T(128)}, u32[]{:S(2)}) copy-start(s32[25]{0:T(128)} %constant.263) | copy-start | bytes 304
  16.0 31.4 %collective-permute-start.1 = (f32[25,2,256]{2,0,1:T(8,128)S(1)}, f32[25,2,256]{2,0,1:T(8,128)S(1)}, u32[]{:S(2)}, u32[]{:S(2)}) collective-permute-start(f32[25,2,256]{2,0,1:T(8,128)S(1)} %bitcast.204), channel_id=1, source_target_pairs={{2,0},{4,2},{6,4},{8,6},{10,8},{12,10},{14,12},{16,14},{18,16},{20... | collective-permute-start | bytes 153608 | tf_op jit(solution)/shard_map/ppermute | solution.py:23
  22.2 1.4 copy-start.22
  22.3 1.4 copy-start.20
  23.5 24.2 %collective-permute-start = (f32[25,2,256]{2,0,1:T(8,128)S(1)}, f32[25,2,256]{2,0,1:T(8,128)S(1)}, u32[]{:S(2)}, u32[]{:S(2)}) collective-permute-start(f32[25,2,256]{2,0,1:T(8,128)S(1)} %bitcast.205), channel_id=1, source_target_pairs={{30,0},{0,2},{2,4},{4,6},{6,8},{8,10},{10,12},{12,14},{14,16},{16,... | collective-permute-start | bytes 153608 | tf_op jit(solution)/shard_map/ppermute | solution.py:23
  25.2 1.7 copy-start.19
  25.2 1.7 copy-start.18
  25.2 1.7 copy-start.13
  25.8 1.1 copy-start.3
  26.8 0.8 copy-start.4
  26.8 7.8 %collective-permute-start.2 = (f32[25,2,16]{2,0,1:T(8,128)S(1)}, f32[25,2,16]{2,0,1:T(8,128)S(1)}, u32[]{:S(2)}, u32[]{:S(2)}) collective-permute-start(f32[25,2,16]{2,0,1:T(8,128)S(1)} %select_bitcast_fusion.3), channel_id=1, source_target_pairs={{0,1},{1,0},{2,3},{3,2},{4,5},{5,4},{6,7},{7,6},{8,9},{9,8},{10,11... | collective-permute-start | bytes 9608 | tf_op jit(solution)/shard_map/ppermute | solution.py:33
  27.6 0.8 copy-start.5
  28.8 1.3 copy-start.14
  28.9 1.3 copy-start.17
  28.9 1.4 copy-start.6
  30.3 0.8 copy-start.8
  31.1 0.7 copy-start.23
  31.8 0.8 copy-start.7
  32.6 0.7 copy-start.11
  39.0 82.4 %all-to-all-start.2 = ((f32[16,2,14,125]{3,1,2,0:T(2,128)}), f32[16,2,14,125]{3,1,2,0:T(2,128)S(1)}, u32[]{:S(2)}, u32[]{:S(2)}) async-start(f32[16,2,14,125]{3,1,2,0:T(2,128)} %copy.461), calls=%async_computation.2 | async-start | bytes 458752 | tf_op jit(solution)/shard_map/all_to_all | solution.py:140
  48.1 0.9 copy-start.2
  48.1 0.9 copy-start.9
  48.1 1.0 copy-start.10
  48.1 1.0 copy-start.12
  58.0 10.1 %collective-permute-start.5 = (f32[25,2,16]{2,0,1:T(8,128)S(1)}, f32[25,2,16]{2,0,1:T(8,128)S(1)}, u32[]{:S(2)}, u32[]{:S(2)}) collective-permute-start(f32[25,2,16]{2,0,1:T(8,128)S(1)} %select_bitcast_fusion.2), channel_id=1, source_target_pairs={{0,1},{1,0},{2,3},{3,2},{4,5},{5,4},{6,7},{7,6},{8,9},{9,8},{10,11... | collective-permute-start | bytes 9608 | tf_op jit(solution)/shard_map/ppermute | solution.py:33
  61.2 7.6 %collective-permute-start.4 = (f32[25,2,256]{2,0,1:T(8,128)S(1)}, f32[25,2,256]{2,0,1:T(8,128)S(1)}, u32[]{:S(2)}, u32[]{:S(2)}) collective-permute-start(f32[25,2,256]{2,0,1:T(8,128)S(1)} %bitcast.207), channel_id=1, source_target_pairs={{2,0},{4,2},{6,4},{8,6},{10,8},{12,10},{14,12},{16,14},{18,16},{20... | collective-permute-start | bytes 153608 | tf_op jit(solution)/shard_map/ppermute | solution.py:23
  67.8 8.1 %collective-permute-start.3 = (f32[25,2,256]{2,0,1:T(8,128)S(1)}, f32[25,2,256]{2,0,1:T(8,128)S(1)}, u32[]{:S(2)}, u32[]{:S(2)}) collective-permute-start(f32[25,2,256]{2,0,1:T(8,128)S(1)} %bitcast.208), channel_id=1, source_target_pairs={{30,0},{0,2},{2,4},{4,6},{6,8},{8,10},{10,12},{12,14},{14,16},{16,... | collective-permute-start | bytes 153608 | tf_op jit(solution)/shard_map/ppermute | solution.py:23
  86.0 6.6 %collective-permute-start.8 = (f32[25,2,16]{2,0,1:T(8,128)S(1)}, f32[25,2,16]{2,0,1:T(8,128)S(1)}, u32[]{:S(2)}, u32[]{:S(2)}) collective-permute-start(f32[25,2,16]{2,0,1:T(8,128)S(1)} %select_bitcast_fusion.1), channel_id=1, source_target_pairs={{0,1},{1,0},{2,3},{3,2},{4,5},{5,4},{6,7},{7,6},{8,9},{9,8},{10,11... | collective-permute-start | bytes 9608 | tf_op jit(solution)/shard_map/ppermute | solution.py:33
  89.1 4.5 %collective-permute-start.7 = (f32[25,2,256]{2,0,1:T(8,128)S(1)}, f32[25,2,256]{2,0,1:T(8,128)S(1)}, u32[]{:S(2)}, u32[]{:S(2)}) collective-permute-start(f32[25,2,256]{2,0,1:T(8,128)S(1)} %bitcast.209), channel_id=1, source_target_pairs={{2,0},{4,2},{6,4},{8,6},{10,8},{12,10},{14,12},{16,14},{18,16},{20... | collective-permute-start | bytes 153608 | tf_op jit(solution)/shard_map/ppermute | solution.py:23
  90.2 8.4 %collective-permute-start.6 = (f32[25,2,256]{2,0,1:T(8,128)S(1)}, f32[25,2,256]{2,0,1:T(8,128)S(1)}, u32[]{:S(2)}, u32[]{:S(2)}) collective-permute-start(f32[25,2,256]{2,0,1:T(8,128)S(1)} %bitcast.210), channel_id=1, source_target_pairs={{30,0},{0,2},{2,4},{4,6},{6,8},{8,10},{10,12},{12,14},{14,16},{16,... | collective-permute-start | bytes 153608 | tf_op jit(solution)/shard_map/ppermute | solution.py:23
  108.6 6.3 %collective-permute-start.11 = (f32[25,2,16]{2,0,1:T(8,128)S(1)}, f32[25,2,16]{2,0,1:T(8,128)S(1)}, u32[]{:S(2)}, u32[]{:S(2)}) collective-permute-start(f32[25,2,16]{2,0,1:T(8,128)S(1)} %select_bitcast_fusion), channel_id=1, source_target_pairs={{0,1},{1,0},{2,3},{3,2},{4,5},{5,4},{6,7},{7,6},{8,9},{9,8},{10,11... | collective-permute-start | bytes 9608 | tf_op jit(solution)/shard_map/ppermute | solution.py:33
  111.8 13.2 %collective-permute-start.10 = (f32[25,2,256]{2,0,1:T(8,128)S(1)}, f32[25,2,256]{2,0,1:T(8,128)S(1)}, u32[]{:S(2)}, u32[]{:S(2)}) collective-permute-start(f32[25,2,256]{2,0,1:T(8,128)S(1)} %bitcast.206), channel_id=1, source_target_pairs={{2,0},{4,2},{6,4},{8,6},{10,8},{12,10},{14,12},{16,14},{18,16},{20... | collective-permute-start | bytes 153608 | tf_op jit(solution)/shard_map/ppermute | solution.py:23
  112.9 8.1 %collective-permute-start.9 = (f32[25,2,256]{2,0,1:T(8,128)S(1)}, f32[25,2,256]{2,0,1:T(8,128)S(1)}, u32[]{:S(2)}, u32[]{:S(2)}) collective-permute-start(f32[25,2,256]{2,0,1:T(8,128)S(1)} %bitcast.211), channel_id=1, source_target_pairs={{30,0},{0,2},{2,4},{4,6},{6,8},{8,10},{10,12},{12,14},{14,16},{16,... | collective-permute-start | bytes 153608 | tf_op jit(solution)/shard_map/ppermute | solution.py:23
  121.4 12.9 %all-to-all-start.4 = ((f32[16,2,14,125]{3,1,2,0:T(2,128)}), f32[16,2,14,125]{3,1,2,0:T(2,128)S(1)}, u32[]{:S(2)}, u32[]{:S(2)}) async-start(f32[16,2,14,125]{3,1,2,0:T(2,128)} %copy.464), calls=%async_computation.4 | async-start | bytes 458752 | tf_op jit(solution)/shard_map/all_to_all | solution.py:140
  134.3 5.0 %all-to-all-start.3 = ((f32[16,2,14,125]{3,0,2,1:T(8,128)}), f32[16,2,14,125]{3,0,2,1:T(8,128)S(1)}, u32[]{:S(2)}, u32[]{:S(2)}) async-start(f32[16,2,14,125]{3,0,2,1:T(8,128)} %copy.462), calls=%async_computation.3 | async-start | bytes 458752 | tf_op jit(solution)/shard_map/all_to_all | solution.py:139
  143.2 13.3 %all-to-all-start.6 = ((f32[16,2,14,125]{3,1,2,0:T(2,128)}), f32[16,2,14,125]{3,1,2,0:T(2,128)S(1)}, u32[]{:S(2)}, u32[]{:S(2)}) async-start(f32[16,2,14,125]{3,1,2,0:T(2,128)} %copy.467), calls=%async_computation.6 | async-start | bytes 458752 | tf_op jit(solution)/shard_map/all_to_all | solution.py:140
  160.4 13.3 %all-to-all-start.8 = ((f32[16,2,14,125]{3,1,2,0:T(2,128)}), f32[16,2,14,125]{3,1,2,0:T(2,128)S(1)}, u32[]{:S(2)}, u32[]{:S(2)}) async-start(f32[16,2,14,125]{3,1,2,0:T(2,128)} %copy.470), calls=%async_computation.8 | async-start | bytes 458752 | tf_op jit(solution)/shard_map/all_to_all | solution.py:140
where the time goes:
time: 180 us; the launch traced here: 179 us
  starting transfers between devices  45.5 us (25%)
  local copies, waits for them, and re-layouts  45 us (25%)
  waiting for transfers between devices  43.8 us (24%)
  matrix products  22 us (12%)
  blocking collectives  15.4 us (9%)
  other arithmetic  4.98 us (3%)
  between operations  2.14 us (1%)
    all_to_all x4, waiting for transfers between devices, per_device(): lax.all_to_all(blocks.reshape(groups, layers, capacity, NODES), 'group',...  24.7 us
    ppermute x8, waiting for transfers between devices, from_behind(): return lax.ppermute(block, axis, route)  17.6 us
    all_to_all x4, starting transfers between devices, per_device(): lax.all_to_all(blocks.reshape(groups, layers, capacity, NODES), 'group',...  17.6 us
    gather x48, local copies, waits for them, and re-layouts, per_device(): faces = [jnp.take(state, row_ids[f], axis=0) for f in range(6)]  16.2 us
    ppermute x8, starting transfers between devices, from_behind(): return lax.ppermute(block, axis, route)  15.9 us
    all_to_all x3, blocking collectives, per_device(): lax.all_to_all(lax.all_to_all(blocks.reshape(groups, layers, capacity, NO...  11.7 us
    dot_general x28, matrix products, apply_nodes(): jnp.einsum('mn,n...->m...', jnp.asarray(matrix, jnp.float32), field, prec...  11.4 us
    all_to_all x1, starting transfers between devices, per_device(): lax.all_to_all(labels, 'group', split_axis=0, concat_axis=0, tiled=True)  8.31 us
  transfers between devices with their start and end apart: 18, of which 8 were waited for; matrix products, arithmetic and copies ran while one was open for 36% of the time, Pallas kernels for 0%

commit v1 on v0

v1 whole, which is shorter than its diff:
```python
import functools
import math

import jax
import jax.numpy as jnp
import numpy as np
from jax import lax
from jax.experimental import pallas as pl
from jax.experimental.pallas import tpu as pltpu
from jax.sharding import PartitionSpec as P

NODES = 125
STEPS = 4
P_DEV = 128
ROWS = 128
FACE = 32

PENALTY = 40.0
DT_SQUARED = 0.001
KERNEL_SCALE = 0.05
MESH = pl.DeviceIdType.MESH
F32, BF16 = jnp.float32, jnp.bfloat16
LOW, HIGH, RADIAL, OWNER, SLOT, TABLE = 6, 7, 8, 9, 10, 16


def gll_tables():
    points = np.array([-1.0, -math.sqrt(3.0 / 7.0), 0.0, math.sqrt(3.0 / 7.0), 1.0])
    weights = np.array([0.1, 49.0 / 90.0, 32.0 / 45.0, 49.0 / 90.0, 0.1])
    barycentric = np.array(
        [np.prod([points[i] - points[m] for m in range(5) if m != i]) for i in range(5)]
    )
    derivative = np.zeros((5, 5))
    for i in range(5):
        for j in range(5):
            if i != j:
                derivative[i, j] = barycentric[i] / (barycentric[j] * (points[i] - points[j]))
            else:
                derivative[i, j] = sum((1.0 / (points[i] - points[m]) for m in range(5) if m != i))
    return (weights, derivative)


def padded(matrix, rows, columns):
    out = np.zeros((rows, columns))
    out[: matrix.shape[0], : matrix.shape[1]] = matrix
    return out


def constants():
    weights, derivative = gll_tables()
    one = np.eye(5)
    grads = [
        np.kron(derivative, np.kron(one, one)),
        np.kron(one, np.kron(derivative, one)),
        np.kron(one, np.kron(one, derivative)),
    ]
    cube = np.kron(weights, np.kron(weights, weights))
    stiff = sum(g.T @ (cube[:, None] * g) for g in grads) / cube[:, None]
    digits = [(n // 25, n // 5 % 5, n % 5) for n in range(NODES)]
    nodes_of = []
    for f in range(6):
        level = 0 if f % 2 == 0 else 4
        nodes_of.append([n for n in range(NODES) if digits[n][f // 2] == level])
    blocks = [padded(m, ROWS, ROWS) for m in grads + [stiff]]
    spread = np.zeros((ROWS, 4 * 2 * FACE))
    for f in range(2, 6):
        pick = np.zeros((FACE, ROWS))
        for a, n in enumerate(nodes_of[f]):
            pick[a, n] = 1.0
            spread[n, (f - 2) * 2 * FACE + a] = 1.0
            spread[n, (f - 2) * 2 * FACE + FACE + a] = 1.0
        blocks.append(pick)
    operator = np.concatenate(blocks, axis=0).astype(np.float32)
    bf = jnp.bfloat16
    high = operator.astype(bf)
    low = (operator - high.astype(np.float32)).astype(bf)
    operator = np.concatenate([high, high, low], axis=1)
    factor = np.zeros((2 * ROWS, 128), np.float32)
    faces = np.array([sum(n in set(nodes_of[f]) for f in range(6)) for n in range(NODES)])
    edge = DT_SQUARED * PENALTY / weights[0]
    factor[:NODES] = (2.0 - edge * faces)[:, None]
    factor[ROWS : ROWS + NODES] = (KERNEL_SCALE * cube)[:, None]
    return operator, spread.astype(bf), factor, edge


def split(values):
    high = values.astype(BF16)
    return high, (values - high.astype(F32)).astype(BF16)


def dot(a, b):
    return jnp.dot(a, b, preferred_element_type=F32)


def onehot(row, count, offset=0):
    places = lax.broadcasted_iota(jnp.int32, (count, row.shape[1]), 0) + offset
    return jnp.where(places == row, 1.0, 0.0).astype(BF16)


def stacked(face, elements):
    high, low = split(face)
    return jnp.concatenate(
        [high[:, :elements], high[:, elements:], low[:, :elements], low[:, elements:]], axis=0
    )


def summed(found):
    total = found[: 2 * FACE] + found[2 * FACE :]
    return jnp.concatenate([total[:FACE], total[FACE:]], axis=1)


def kernel(
    sizes,
    edge,
    fwd_now,
    fwd_prev,
    adj_now,
    adj_prev,
    speed,
    table,
    owner,
    operator,
    spread,
    factor,
    fwd_out,
    adj_out,
    grad_out,
    state,
    previous,
    total,
    picks,
    halo_picks,
    peer_table,
    sent,
    got,
    blocks,
    got_blocks,
    table_send,
    table_recv,
    face_send,
    face_recv,
    block_send,
    block_recv,
):
    groups, layers, elements, capacity, room = sizes
    devices = groups * layers
    both = 2 * elements
    group, layer = lax.axis_index("group"), lax.axis_index("depth")
    me = group * layers + layer
    right = (lax.rem(group + 1, groups), layer)
    left = (lax.rem(group + groups - 1, groups), layer)
    across = (group, 1 - layer)
    partners = (right, left, across)

    barrier = pltpu.get_barrier_semaphore()

    def at(number):
        return (number // layers, lax.rem(number, layers))

    def greet(k, carry):
        other = lax.rem(me + k, devices)
        pl.semaphore_signal(barrier, inc=1, device_id=at(other), device_id_type=MESH)
        return carry

    lax.fori_loop(1, devices, greet, 0)

    state[ROWS - 8 :, :] = jnp.zeros((8, both), F32)
    previous[ROWS - 8 :, :] = jnp.zeros((8, both), F32)
    state[:NODES, :elements] = fwd_now[...]
    state[:NODES, elements:] = adj_now[...]
    previous[:NODES, :elements] = fwd_prev[...]
    previous[:NODES, elements:] = adj_prev[...]
    total[...] = jnp.zeros_like(total)

    def table_copy(side):
        return pltpu.make_async_remote_copy(
            src_ref=table,
            dst_ref=peer_table.at[side],
            send_sem=table_send.at[side],
            recv_sem=table_recv.at[side],
            device_id=partners[side],
            device_id_type=MESH,
        )

    def face_copy(side, step):
        return pltpu.make_async_remote_copy(
            src_ref=sent.at[side, step],
            dst_ref=got.at[side, step],
            send_sem=face_send.at[side, step],
            recv_sem=face_recv.at[side, step],
            device_id=partners[side],
            device_id_type=MESH,
        )

    def block_copy(k):
        other = lax.rem(me + k, devices)
        return pltpu.make_async_remote_copy(
            src_ref=blocks.at[other],
            dst_ref=got_blocks.at[me],
            send_sem=block_send.at[other],
            recv_sem=block_recv.at[me],
            device_id=at(other),
            device_id_type=MESH,
        )

    def block_arrival(k):
        other = lax.rem(me + k, devices)
        return pltpu.make_async_remote_copy(
            src_ref=blocks.at[other],
            dst_ref=got_blocks.at[other],
            send_sem=block_send.at[other],
            recv_sem=block_recv.at[other],
            device_id=at(other),
            device_id_type=MESH,
        )

    rows = lax.broadcasted_iota(jnp.int32, (FACE, both), 0)

    def fill(step):
        top = pltpu.roll(state[ROWS - FACE :, :], FACE - 4, 0)
        sent[0, step] = jnp.where(rows < 25, top, 0.0)
        bottom = pltpu.roll(state[:FACE, :], 4, 0)
        sent[1, step] = jnp.where((rows >= 4) & (rows < 29), bottom, 0.0)
        first = pl.multiple_of(4 * ROWS + 3 * FACE - FACE * layer, FACE)
        high, low = split(state[...])
        pick = operator[pl.ds(first, FACE), : 2 * ROWS]
        sent[2, step] = dot(pick, jnp.concatenate([high, low], axis=0))

    fill(0)
    pl.semaphore_wait(barrier, devices - 1)
    for side in range(3):
        table_copy(side).start()
        face_copy(side, 0).start()

    lists = table[...]
    for f in range(6):
        picks[f] = onehot(lists[f : f + 1], elements)
    before = (owner[...] == lists[OWNER : OWNER + 1]) & (
        lax.broadcasted_iota(jnp.int32, (elements, elements), 0)
        < lax.broadcasted_iota(jnp.int32, (elements, elements), 1)
    )
    position = jnp.sum(jnp.where(before, 1.0, 0.0), axis=0, keepdims=True).astype(jnp.int32)
    placing = lists[OWNER : OWNER + 1] * room + position

    for side in range(3):
        table_copy(side).wait_recv()
    for slot, (side, row, f) in enumerate(
        ((0, HIGH, 0), (1, LOW, 1), (2, RADIAL, 4), (2, RADIAL, 5))
    ):
        theirs = onehot(peer_table[side, row : row + 1], elements)
        mine = onehot(lists[f : f + 1], elements, elements)
        halo_picks[slot] = dot(theirs, mine).astype(BF16)

    speeds = jnp.concatenate([speed[...], speed[...]], axis=1)
    wide = both // 128

    def advance(step, carry):
        high, low = split(state[...])
        parts = dot(operator[...], jnp.concatenate([high, low, high], axis=0))
        product = total[...]
        for d in range(3):
            one = parts[d * ROWS : (d + 1) * ROWS]
            product = product + one[:, :elements] * one[:, elements:]
        total[...] = product

        @pl.when(step == STEPS - 1)
        def _():
            scale = jnp.concatenate([factor[ROWS:]] * (elements // 128), axis=1)
            block = scale * speed[...] * total[...]
            node = lax.broadcasted_iota(jnp.int32, (ROWS, elements), 0)
            label = (lists[SLOT : SLOT + 1] + 1).astype(F32)
            block = jnp.where(node == NODES, label, block)
            block_high, block_low = split(block)
            placer = onehot(placing, devices * room)
            across_nodes = (((1,), (1,)), ((), ()))
            placed = lax.dot_general(placer, block_high, across_nodes, preferred_element_type=F32)
            placed += lax.dot_general(placer, block_low, across_nodes, preferred_element_type=F32)
            blocks[...] = placed.reshape(devices, room, ROWS)

            def start(k, inner):
                block_copy(k).start()
                return inner

            lax.fori_loop(1, devices, start, 0)

        face = [None, None] + [
            stacked(parts[4 * ROWS + f * FACE : 4 * ROWS + (f + 1) * FACE], elements)
            for f in range(4)
        ]
        found = [None, None, dot(face[3], picks[2]), dot(face[2], picks[3])]
        own_low = dot(stacked(sent[0, step], elements), picks[0])
        own_high = dot(stacked(sent[1, step], elements), picks[1])
        face_copy(2, step).wait_recv()
        radial = stacked(got[2, step], elements)
        found.append(dot(face[5], picks[4]) + dot(radial, halo_picks[2]))
        found.append(dot(face[4], picks[5]) + dot(radial, halo_picks[3]))
        pieces = []
        for f in range(2, 6):
            one = found[f].astype(BF16)
            for half in range(2):
                base = 2 * FACE * half
                pieces.append(
                    jnp.concatenate(
                        [one[base : base + FACE], one[base + FACE : base + 2 * FACE]], axis=1
                    )
                )
        penal = dot(spread[...], jnp.concatenate(pieces, axis=0))
        diagonal = jnp.concatenate([factor[:ROWS]] * wide, axis=1)
        now = state[...]
        following = diagonal * now - previous[...]
        following -= DT_SQUARED * speeds * parts[3 * ROWS : 4 * ROWS]
        following += edge * penal
        previous[...] = now
        face_copy(0, step).wait_recv()
        face_copy(1, step).wait_recv()
        low_face = summed(own_low + dot(stacked(got[0, step], elements), halo_picks[0]))
        high_face = summed(own_high + dot(stacked(got[1, step], elements), halo_picks[1]))
        state[:FACE, :] = following[:FACE] + edge * low_face
        state[FACE : ROWS - FACE, :] = following[FACE : ROWS - FACE]
        state[ROWS - FACE :, :] = following[ROWS - FACE :] + edge * high_face

        @pl.when(step < STEPS - 1)
        def _():
            fill(step + 1)
            for side in range(3):
                face_copy(side, step + 1).start()

        return carry

    lax.fori_loop(0, STEPS, advance, 0)

    fwd_out[...] = state[:NODES, :elements]
    adj_out[...] = state[:NODES, elements:]

    got_blocks[me] = blocks[me]

    def arrive(k, carry):
        block_arrival(k).wait_recv()
        return carry

    lax.fori_loop(1, devices, arrive, 0)
    arrived = got_blocks[...].reshape(devices * room, ROWS)
    cell = lax.broadcasted_iota(jnp.int32, (devices * room, P_DEV), 1) + 1
    chosen = jnp.where(arrived[:, NODES : NODES + 1] == cell.astype(F32), 1.0, 0.0)
    chosen = jnp.transpose(chosen).astype(BF16)
    arrived_high, arrived_low = split(arrived)
    grad = dot(chosen, arrived_high) + dot(chosen, arrived_low)
    grad_out[...] = grad[:, :NODES]

    def sent_off(k, carry):
        block_copy(k).wait_send()
        return carry

    lax.fori_loop(1, devices, sent_off, 0)
    for side in range(3):
        table_copy(side).wait_send()
        for step in range(STEPS):
            face_copy(side, step).wait_send()


def per_device(
    fwd_now,
    fwd_prev,
    adj_now,
    adj_prev,
    speed_sq,
    face_lists,
    send_low,
    send_high,
    send_radial,
    owner_dev,
    param_slot,
):
    operator, spread, factor, edge = constants()
    elements = fwd_now.shape[1]
    groups = lax.axis_size("group")
    layers = lax.axis_size("depth")
    devices = groups * layers
    capacity = elements // devices + elements // (2 * devices) + 2
    room = -(-capacity // 8) * 8
    both = 2 * elements

    def row(values):
        return jnp.pad(values, (0, elements - values.shape[0]), constant_values=-1)[None, :]

    table = jnp.concatenate(
        [
            face_lists,
            row(send_low),
            row(send_high),
            row(send_radial),
            owner_dev[:, 0][None, :],
            param_slot[None, :],
            jnp.zeros((TABLE - 11, elements), jnp.int32),
        ],
        axis=0,
    )
    vmem = pl.BlockSpec(memory_space=pltpu.VMEM)
    dma = pltpu.SemaphoreType.DMA
    return pl.pallas_call(
        functools.partial(kernel, (groups, layers, elements, capacity, room), edge),
        out_shape=(
            jax.ShapeDtypeStruct((NODES, elements), F32),
            jax.ShapeDtypeStruct((NODES, elements), F32),
            jax.ShapeDtypeStruct((P_DEV, NODES), F32),
        ),
        in_specs=[vmem] * 10,
        out_specs=(vmem, vmem, vmem),
        scratch_shapes=[
            pltpu.VMEM((ROWS, both), F32),
            pltpu.VMEM((ROWS, both), F32),
            pltpu.VMEM((ROWS, elements), F32),
            pltpu.VMEM((6, elements, elements), BF16),
            pltpu.VMEM((4, elements, elements), BF16),
            pltpu.VMEM((3, TABLE, elements), jnp.int32),
            pltpu.VMEM((3, STEPS, FACE, both), F32),
            pltpu.VMEM((3, STEPS, FACE, both), F32),
            pltpu.VMEM((devices, room, ROWS), F32),
            pltpu.VMEM((devices, room, ROWS), F32),
            dma((3,)),
            dma((3,)),
            dma((3, STEPS)),
            dma((3, STEPS)),
            dma((devices,)),
            dma((devices,)),
        ],
        compiler_params=pltpu.CompilerParams(
            collective_id=0, has_side_effects=True, vmem_limit_bytes=40 * 2**20
        ),
    )(
        fwd_now,
        fwd_prev,
        adj_now,
        adj_prev,
        speed_sq[None, :],
        table,
        owner_dev,
        jnp.asarray(operator),
        jnp.asarray(spread),
        jnp.asarray(factor),
    )


def solution(mesh):
    return jax.shard_map(
        per_device,
        mesh=mesh,
        in_specs=(
            P(None, ("group", "depth")),
            P(None, ("group", "depth")),
            P(None, ("group", "depth")),
            P(None, ("group", "depth")),
            P(("group", "depth")),
            P(None, ("group", "depth")),
            P(("group", "depth")),
            P(("group", "depth")),
            P(("group", "depth")),
            P(("group", "depth"), None),
            P(("group", "depth")),
        ),
        out_specs=(
            P(None, ("group", "depth")),
            P(None, ("group", "depth")),
            P(("group", "depth"), None),
        ),
        check_vma=False,
    )
```

time: 180 us -> 43.3 us (0.24)
  starting transfers between devices: 45.5 us -> 0 us
  waiting for transfers between devices: 43.8 us -> 0 us
  local copies, waits for them, and re-layouts: 45 us -> 10.4 us
  Pallas kernels: 0 us -> 31.9 us
  matrix products: 22 us -> 0 us
  blocking collectives: 15.4 us -> 0 us
  other arithmetic: 4.98 us -> 0 us
    pallas_call x0 -> x1, Pallas kernels: none -> 31.9 us  [per_device(): pl.pallas_call(functools.partial(kernel, (groups, layers, elements, capac...]
    gather x80 -> x0, local copies, waits for them, and re-layouts: 30.5 us -> none  [the longest x48 16.2 us: per_device(): faces = [jnp.take(state, row_ids[f], axis=0) for f in range(6)]]
    all_to_all x6 -> x0, starting transfers between devices: 29.3 us -> none  [the longest x4 17.6 us: per_device(): lax.all_to_all(blocks.reshape(groups, layers, capacity, NODES), 'group',...]
    all_to_all x6 -> x0, waiting for transfers between devices: 26.2 us -> none  [the longest x4 24.7 us: per_device(): lax.all_to_all(blocks.reshape(groups, layers, capacity, NODES), 'group',...]
    dot_general x61 -> x0, matrix products: 22 us -> none  [the longest x28 11.4 us: apply_nodes(): jnp.einsum('mn,n...->m...', jnp.asarray(matrix, jnp.float32), field, prec...]
    ppermute x12 -> x0, waiting for transfers between devices: 17.6 us -> none  [the longest x8 17.6 us: from_behind(): return lax.ppermute(block, axis, route)]
    ppermute x12 -> x0, starting transfers between devices: 16.2 us -> none  [the longest x8 15.9 us: from_behind(): return lax.ppermute(block, axis, route)]
    all_to_all x4 -> x0, blocking collectives: 15.4 us -> none  [the longest x3 11.7 us: per_device(): lax.all_to_all(lax.all_to_all(blocks.reshape(groups, layers, capacity, NO...]
  transfers between devices with their start and end apart: 18 -> 0, of which waited for: 8 -> 0; matrix products, arithmetic and copies ran while one was open for 36% -> 0% of each run, Pallas kernels for 0% -> 0%
where the time goes in v1:
time: 43.3 us; the launch traced here: 43 us
  Pallas kernels  31.9 us (74%)
  local copies, waits for them, and re-layouts  10.4 us (24%)
  between operations  0.7 us (2%)
    pallas_call x1, Pallas kernels, per_device(): pl.pallas_call(functools.partial(kernel, (groups, layers, elements, capac...  31.9 us
    unnamed x22, local copies, waits for them, and re-layouts  8.25 us
    concatenate x1, local copies, waits for them, and re-layouts, per_device(): jnp.concatenate([face_lists, row(send_low), row(send_high), row(send_radi...  1.42 us

profile of v1, /device:TPU:0, one launch (start us, length us, event | category | flops | bytes accessed | tf_op | source)
XLA Modules:
  0.0 43.0 jit_solution(17649030705052217198)
XLA Ops:
  0.6 0.0 copy-start.8
  0.6 0.0 copy-start.1
  0.7 0.7 %pad.4 = s32[256]{0:T(256)S(1)} pad(s32[16]{0:T(128)} %param.22, s32[]{:T(128)} %constant.3.clone.1), padding=0_240 | pad | bytes 1092 | tf_op jit(solution)/shard_map/jit(_pad)/pad | solution.py:383
  1.3 0.0 copy-done.8
  1.4 1.4 %concatenate.3.table = s32[16,256]{1,0:T(8,128)S(1)} concatenate(s32[6,256]{1,0:T(8,128)S(1)} %copy-done.8, s32[1,256]{1,0:T(1,128)} %bitcast.9, s32[1,256]{1,0:T(1,128)} %bitcast.10, s32[1,256]{1,0:T(1,128)S(1)} %bitcast.8, s32[1,256]{1,0:T(1,128)} %bitcast.7, s32[1,256]{1,0:T(1,128)} %bitcast.11, s32[5,256]{1,0:T(8,128)S(1)} %broadcast_in_dim.23), dimensions={0} | concatenate | bytes 32768 | tf_op jit(solution)/shard_map/concatenate | solution.py:385
  2.8 0.0 copy-start.7
  2.8 0.8 %copy.17.owner = s32[256,1]{1,0:T(8,128)S(1)} copy(s32[256,1]{0,1:T(1,128)} %param.23) | data formatting | bytes 2048 | tf_op args[9]
  3.6 0.0 copy-done.1
  3.6 0.0 copy-done.7
  3.6 0.0 copy-start
  3.6 1.0 %copy-done = bf16[640,384]{1,0:T(8,128)(2,1)S(1)} copy-done((bf16[640,384]{1,0:T(8,128)(2,1)S(1)}, bf16[640,384]{1,0:T(8,128)(2,1)}, u32[]{:S(2)}) %copy-start) | copy-done | bytes 491544
  4.7 0.0 copy-start.2
  4.7 0.9 %copy-done.2 = f32[125,256]{1,0:T(8,128)S(1)} copy-done((f32[125,256]{1,0:T(8,128)S(1)}, f32[125,256]{1,0:T(8,128)}, u32[]{:S(2)}) %copy-start.2) | copy-done | bytes 128024
  5.6 0.0 copy-start.3
  5.6 0.9 %copy-done.3 = f32[125,256]{1,0:T(8,128)S(1)} copy-done((f32[125,256]{1,0:T(8,128)S(1)}, f32[125,256]{1,0:T(8,128)}, u32[]{:S(2)}) %copy-start.3) | copy-done | bytes 128024
  6.5 0.0 copy-start.4
  6.5 0.9 %copy-done.4 = f32[125,256]{1,0:T(8,128)S(1)} copy-done((f32[125,256]{1,0:T(8,128)S(1)}, f32[125,256]{1,0:T(8,128)}, u32[]{:S(2)}) %copy-start.4) | copy-done | bytes 128024
  7.4 0.0 copy-start.5
  7.4 0.9 %copy-done.5 = f32[256,128]{1,0:T(8,128)S(1)} copy-done((f32[256,128]{1,0:T(8,128)S(1)}, f32[256,128]{1,0:T(8,128)}, u32[]{:S(2)}) %copy-start.5) | copy-done | bytes 131096
  8.3 0.0 copy-start.6
  8.3 0.8 %copy-done.6 = bf16[128,256]{1,0:T(8,128)(2,1)S(1)} copy-done((bf16[128,256]{1,0:T(8,128)(2,1)S(1)}, bf16[128,256]{1,0:T(8,128)(2,1)}, u32[]{:S(2)}) %copy-start.6) | copy-done | bytes 65560
  9.1 31.9 %shard_map.157 = (f32[125,256]{1,0:T(8,128)S(1)}, f32[125,256]{1,0:T(8,128)S(1)}, f32[128,125]{1,0:T(8,128)S(1)}) custom-call(f32[125,256]{1,0:T(8,128)S(1)} %copy-done.1, f32[125,256]{1,0:T(8,128)S(1)} %copy-done.2, f32[125,256]{1,0:T(8,128)S(1)} %copy-done.3, f32[125,256]{1,0:T(8,128)S(1)} %copy-done.4, f32[1,256]{1,0:T(1,128)S(1)} %bitcast.6, ...), custom_call_target="tpu_custom_call" | custom-call | tf_op jit(solution)/shard_map/pallas_call | solution.py:399
  41.1 0.7 %copy.21 = f32[125,256]{1,0:T(8,128)} copy(f32[125,256]{1,0:T(8,128)S(1)} %get-tuple-element.6) | data formatting | bytes 256000
  41.7 0.7 %copy.22 = f32[125,256]{1,0:T(8,128)} copy(f32[125,256]{1,0:T(8,128)S(1)} %get-tuple-element.7) | data formatting | bytes 256000
  42.4 0.6 %copy.23 = f32[128,125]{1,0:T(8,128)} copy(f32[128,125]{1,0:T(8,128)S(1)} %get-tuple-element.8) | data formatting | bytes 128000
  (1 shorter events, 0.0 us)
Async XLA Ops:
  0.6 0.7 %copy-start.8 = (s32[6,256]{1,0:T(8,128)S(1)}, s32[6,256]{1,0:T(8,128)}, u32[]{:S(2)}) copy-start(s32[6,256]{1,0:T(8,128)} %param.19) | copy-start | bytes 18436
  0.6 3.0 %copy-start.1 = (f32[125,256]{1,0:T(8,128)S(1)}, f32[125,256]{1,0:T(8,128)}, u32[]{:S(2)}) copy-start(f32[125,256]{1,0:T(8,128)} %fwd_now.1) | copy-start | bytes 384004
  2.8 0.8 %copy-start.7 = (f32[256]{0:T(256)S(1)}, f32[256]{0:T(256)}, u32[]{:S(2)}) copy-start(f32[256]{0:T(256)} %param.18) | copy-start | bytes 3076
  3.6 1.0 %copy-start = (bf16[640,384]{1,0:T(8,128)(2,1)S(1)}, bf16[640,384]{1,0:T(8,128)(2,1)}, u32[]{:S(2)}) copy-start(bf16[640,384]{1,0:T(8,128)(2,1)} %constant.10.clone.operator) | copy-start | bytes 1474564
  4.7 0.9 %copy-start.2 = (f32[125,256]{1,0:T(8,128)S(1)}, f32[125,256]{1,0:T(8,128)}, u32[]{:S(2)}) copy-start(f32[125,256]{1,0:T(8,128)} %fwd_prev.1) | copy-start | bytes 384004
  5.6 0.9 %copy-start.3 = (f32[125,256]{1,0:T(8,128)S(1)}, f32[125,256]{1,0:T(8,128)}, u32[]{:S(2)}) copy-start(f32[125,256]{1,0:T(8,128)} %adj_now.1) | copy-start | bytes 384004
  6.5 0.9 %copy-start.4 = (f32[125,256]{1,0:T(8,128)S(1)}, f32[125,256]{1,0:T(8,128)}, u32[]{:S(2)}) copy-start(f32[125,256]{1,0:T(8,128)} %adj_prev.1) | copy-start | bytes 384004
  7.4 0.9 %copy-start.5 = (f32[256,128]{1,0:T(8,128)S(1)}, f32[256,128]{1,0:T(8,128)}, u32[]{:S(2)}) copy-start(f32[256,128]{1,0:T(8,128)} %constant.12.clone.factor) | copy-start | bytes 393220
  8.3 0.8 %copy-start.6 = (bf16[128,256]{1,0:T(8,128)(2,1)S(1)}, bf16[128,256]{1,0:T(8,128)(2,1)}, u32[]{:S(2)}) copy-start(bf16[128,256]{1,0:T(8,128)(2,1)} %constant.11.clone.spread) | copy-start | bytes 196612

commit v2 on v1

v2 whole, which is shorter than its diff:
```python
import functools
import math

import jax
import jax.numpy as jnp
import numpy as np
from jax import lax
from jax.experimental import pallas as pl
from jax.experimental.pallas import tpu as pltpu
from jax.sharding import PartitionSpec as P

NODES = 125
STEPS = 4
P_DEV = 128
ROWS = 128
FACE = 32

PENALTY = 40.0
DT_SQUARED = 0.001
KERNEL_SCALE = 0.05
MESH = pl.DeviceIdType.MESH
F32, BF16 = jnp.float32, jnp.bfloat16


def gll_tables():
    points = np.array([-1.0, -math.sqrt(3.0 / 7.0), 0.0, math.sqrt(3.0 / 7.0), 1.0])
    weights = np.array([0.1, 49.0 / 90.0, 32.0 / 45.0, 49.0 / 90.0, 0.1])
    barycentric = np.array(
        [np.prod([points[i] - points[m] for m in range(5) if m != i]) for i in range(5)]
    )
    derivative = np.zeros((5, 5))
    for i in range(5):
        for j in range(5):
            if i != j:
                derivative[i, j] = barycentric[i] / (barycentric[j] * (points[i] - points[j]))
            else:
                derivative[i, j] = sum((1.0 / (points[i] - points[m]) for m in range(5) if m != i))
    return (weights, derivative)


def padded(matrix, rows, columns):
    out = np.zeros((rows, columns))
    out[: matrix.shape[0], : matrix.shape[1]] = matrix
    return out


def constants():
    weights, derivative = gll_tables()
    one = np.eye(5)
    grads = [
        np.kron(derivative, np.kron(one, one)),
        np.kron(one, np.kron(derivative, one)),
        np.kron(one, np.kron(one, derivative)),
    ]
    cube = np.kron(weights, np.kron(weights, weights))
    stiff = sum(g.T @ (cube[:, None] * g) for g in grads) / cube[:, None]
    digits = [(n // 25, n // 5 % 5, n % 5) for n in range(NODES)]
    nodes_of = []
    for f in range(6):
        level = 0 if f % 2 == 0 else 4
        nodes_of.append([n for n in range(NODES) if digits[n][f // 2] == level])
    blocks = [padded(m, ROWS, ROWS) for m in grads + [stiff]]
    spread = np.zeros((ROWS, 4 * 2 * FACE))
    for f in range(2, 6):
        pick = np.zeros((FACE, ROWS))
        for a, n in enumerate(nodes_of[f]):
            pick[a, n] = 1.0
            spread[n, (f - 2) * 2 * FACE + a] = 1.0
            spread[n, (f - 2) * 2 * FACE + FACE + a] = 1.0
        blocks.append(pick)
    operator = np.concatenate(blocks, axis=0).astype(np.float32)
    bf = jnp.bfloat16
    high = operator.astype(bf)
    low = (operator - high.astype(np.float32)).astype(bf)
    operator = np.concatenate([high, high, low], axis=1)
    factor = np.zeros((2 * ROWS, 128), np.float32)
    faces = np.array([sum(n in set(nodes_of[f]) for f in range(6)) for n in range(NODES)])
    edge = DT_SQUARED * PENALTY / weights[0]
    factor[:NODES] = (2.0 - edge * faces)[:, None]
    factor[ROWS : ROWS + NODES] = (KERNEL_SCALE * cube)[:, None]
    return operator, spread.astype(bf), factor, edge


def split(values):
    high = values.astype(BF16)
    return high, (values - high.astype(F32)).astype(BF16)


def dot(a, b):
    return jnp.dot(a, b, preferred_element_type=F32)


def onehot(row, count, offset=0):
    places = lax.broadcasted_iota(jnp.int32, (count, row.shape[1]), 0) + offset
    return jnp.where(places == row, 1.0, 0.0).astype(BF16)


def filled(face):
    return jnp.concatenate([face, jnp.zeros((FACE - 25, face.shape[1]), F32)], axis=0)


def stacked(face):
    return jnp.concatenate(split(face), axis=0)


def kernel(
    sizes,
    edge,
    fwd_now,
    fwd_prev,
    adj_now,
    adj_prev,
    speed_in,
    lists_in,
    low_in,
    high_in,
    radial_in,
    owner_in,
    slot_in,
    operator_in,
    spread_in,
    factor_in,
    final,
    grad_out,
    state,
    raw,
    previous,
    following,
    slopes,
    total,
    speed,
    lists,
    owner,
    slot,
    operator,
    spread,
    factor,
    picks,
    halo_picks,
    peer_high,
    peer_low,
    peer_radial,
    sent,
    got,
    blocks,
    got_blocks,
    load_sem,
    table_send,
    table_recv,
    face_send,
    face_recv,
    block_send,
    block_recv,
):
    groups, layers, elements, capacity, room = sizes
    devices = groups * layers
    count = radial_in.shape[1]
    group, layer = lax.axis_index("group"), lax.axis_index("depth")
    me = group * layers + layer
    right = (lax.rem(group + 1, groups), layer)
    left = (lax.rem(group + groups - 1, groups), layer)
    across = (group, 1 - layer)
    partners = (right, left, across)

    loads = [
        pltpu.make_async_copy(source, target, load_sem.at[number])
        for number, (source, target) in enumerate(
            (
                (fwd_now, raw.at[0]),
                (adj_now, raw.at[1]),
                (operator_in, operator),
                (lists_in, lists),
                (owner_in, owner),
                (fwd_prev, raw.at[2]),
                (adj_prev, raw.at[3]),
                (spread_in, spread),
                (factor_in, factor),
                (speed_in, speed),
                (slot_in, slot),
            )
        )
    ]
    state[:, ROWS - 8 :, :] = jnp.zeros((2, 8, elements), F32)
    previous[:, ROWS - 8 :, :] = jnp.zeros((2, 8, elements), F32)
    total[...] = jnp.zeros_like(total)
    for load in loads:
        load.start()

    barrier = pltpu.get_barrier_semaphore()

    def at(number):
        return (number // layers, lax.rem(number, layers))

    def greet(k, carry):
        other = lax.rem(me + k, devices)
        pl.semaphore_signal(barrier, inc=1, device_id=at(other), device_id_type=MESH)
        return carry

    lax.fori_loop(1, devices, greet, 0)

    def table_copy(side):
        return pltpu.make_async_remote_copy(
            src_ref=(high_in, low_in, radial_in)[side],
            dst_ref=(peer_high, peer_low, peer_radial)[side],
            send_sem=table_send.at[side],
            recv_sem=table_recv.at[side],
            device_id=partners[side],
            device_id_type=MESH,
        )

    def face_copy(side, step, field):
        return pltpu.make_async_remote_copy(
            src_ref=sent.at[side, step, field],
            dst_ref=got.at[side, step, field],
            send_sem=face_send.at[side, step, field],
            recv_sem=face_recv.at[side, step, field],
            device_id=partners[side],
            device_id_type=MESH,
        )

    def block_copy(k, arriving=False):
        other = lax.rem(me + k, devices)
        place = other if arriving else me
        return pltpu.make_async_remote_copy(
            src_ref=blocks.at[other],
            dst_ref=got_blocks.at[place],
            send_sem=block_send.at[other],
            recv_sem=block_recv.at[place],
            device_id=at(other),
            device_id_type=MESH,
        )

    def fill_lateral(step, field):
        sent[0, step, field] = state[field, NODES - 25 : NODES, :]
        sent[1, step, field] = state[field, :25, :]

    def fill_radial(step, field):
        first = pl.multiple_of(4 * ROWS + 3 * FACE - FACE * layer, FACE)
        pick = operator[pl.ds(first, FACE), : 2 * ROWS]
        face = dot(pick, jnp.concatenate(split(state[field]), axis=0))
        sent[2, step, field] = face[:25]

    for field in range(2):
        loads[field].wait()
        state[field, :NODES, :] = raw[field]
        fill_lateral(0, field)
    pl.semaphore_wait(barrier, devices - 1)
    for field in range(2):
        face_copy(0, 0, field).start()
        face_copy(1, 0, field).start()
    for side in range(3):
        table_copy(side).start()
    loads[2].wait()
    for field in range(2):
        fill_radial(0, field)
        face_copy(2, 0, field).start()

    loads[3].wait()
    for f in range(6):
        picks[f] = onehot(lists[f : f + 1], elements)
    for load in loads[4:]:
        load.wait()
    for field in range(2):
        previous[field, :NODES, :] = raw[2 + field]

    def prepare(step, field):
        now = state[field]
        high, low = split(now)
        parts = dot(operator[...], jnp.concatenate([high, low, high], axis=0))
        if field == 0:
            slopes[...] = parts[: 3 * ROWS]
        else:
            product = total[...]
            for d in range(3):
                span = slice(d * ROWS, (d + 1) * ROWS)
                product = product + slopes[span] * parts[span]
            total[...] = product

            @pl.when(step == STEPS - 1)
            def _():
                share()

        face = [None, None] + [
            stacked(parts[4 * ROWS + f * FACE : 4 * ROWS + (f + 1) * FACE]) for f in range(4)
        ]
        found = [dot(face[3], picks[2]), dot(face[2], picks[3])]
        fourth, fifth = dot(face[5], picks[4]), dot(face[4], picks[5])
        face_copy(2, step, field).wait_recv()
        radial = stacked(filled(got[2, step, field]))
        found.append(fourth + dot(radial, halo_picks[2]))
        found.append(fifth + dot(radial, halo_picks[3]))
        penal = dot(spread[...], jnp.concatenate([one.astype(BF16) for one in found], axis=0))
        diagonal = jnp.concatenate([factor[:ROWS]] * (elements // 128), axis=1)
        after = diagonal * now - previous[field]
        after -= DT_SQUARED * speed[...] * parts[3 * ROWS : 4 * ROWS]
        following[field] = after + edge * penal
        previous[field] = now

    def lateral(side, step, field):
        found = dot(stacked(filled(sent[side, step, field])), picks[side])
        found += dot(stacked(filled(got[side, step, field])), halo_picks[side])
        return edge * (found[:FACE] + found[FACE:])

    def finish(step, field):
        face_copy(0, step, field).wait_recv()
        face_copy(1, step, field).wait_recv()
        state[field, :FACE, :] = following[field, :FACE, :] + lateral(0, step, field)
        raised = pltpu.roll(lateral(1, step, field), 4, 0)
        state[field, ROWS - FACE :, :] = following[field, ROWS - FACE :, :] + raised
        state[field, FACE : ROWS - FACE, :] = following[field, FACE : ROWS - FACE, :]

    def share():
        before_row = owner[...].astype(F32)
        square = jnp.broadcast_to(before_row, (elements, elements))
        before = (jnp.transpose(square) == square) & (
            lax.broadcasted_iota(jnp.int32, (elements, elements), 0)
            < lax.broadcasted_iota(jnp.int32, (elements, elements), 1)
        )
        position = jnp.sum(jnp.where(before, 1.0, 0.0), axis=0, keepdims=True).astype(jnp.int32)
        placer = onehot(owner[...] * room + position, devices * room)
        scale = jnp.concatenate([factor[ROWS:]] * (elements // 128), axis=1)
        block = scale * speed[...] * total[...]
        node = lax.broadcasted_iota(jnp.int32, (ROWS, elements), 0)
        block = jnp.where(node == NODES, (slot[...] + 1).astype(F32), block)
        block_high, block_low = split(block)
        last = (((1,), (1,)), ((), ()))
        placed = lax.dot_general(placer, block_high, last, preferred_element_type=F32)
        placed += lax.dot_general(placer, block_low, last, preferred_element_type=F32)
        blocks[...] = placed.reshape(devices, room, ROWS)

        def start(k, inner):
            block_copy(k).start()
            return inner

        lax.fori_loop(1, devices, start, 0)

    for side in range(3):
        table_copy(side).wait_recv()
    for place, (theirs, f, many) in enumerate(
        ((peer_high, 0, elements), (peer_low, 1, elements), (peer_radial, 4, count), (peer_radial, 5, count))
    ):
        mine = onehot(lists[f : f + 1], many, elements)
        halo_picks[place] = dot(onehot(theirs[...], elements), mine).astype(BF16)

    prepare(0, 0)
    prepare(0, 1)

    def advance(step, carry):
        for field in range(2):
            finish(step - 1, field)
            fill_lateral(step, field)
            face_copy(0, step, field).start()
            face_copy(1, step, field).start()
            fill_radial(step, field)
            face_copy(2, step, field).start()
            prepare(step, field)
        return carry

    lax.fori_loop(1, STEPS, advance, 0)
    for field in range(2):
        finish(STEPS - 1, field)
        final[field] = state[field, :NODES, :]

    got_blocks[me] = blocks[me]

    def arrive(k, carry):
        block_copy(k, True).wait_recv()
        return carry

    lax.fori_loop(1, devices, arrive, 0)
    arrived = got_blocks[...].reshape(devices * room, ROWS)
    cell = lax.broadcasted_iota(jnp.int32, (devices * room, P_DEV), 1) + 1
    chosen = jnp.where(arrived[:, NODES : NODES + 1] == cell.astype(F32), 1.0, 0.0)
    chosen = jnp.transpose(chosen).astype(BF16)
    arrived_high, arrived_low = split(arrived)
    grad = dot(chosen, arrived_high) + dot(chosen, arrived_low)
    grad_out[...] = grad[:, :NODES]

    def sent_off(k, carry):
        block_copy(k).wait_send()
        return carry

    lax.fori_loop(1, devices, sent_off, 0)
    for side in range(3):
        table_copy(side).wait_send()
        for step in range(STEPS):
            for field in range(2):
                face_copy(side, step, field).wait_send()


def deliver(final, grad, fwd_out, adj_out, grad_out, sem):
    copies = [
        pltpu.make_async_copy(final.at[0], fwd_out, sem.at[0]),
        pltpu.make_async_copy(final.at[1], adj_out, sem.at[1]),
        pltpu.make_async_copy(grad, grad_out, sem.at[2]),
    ]
    for copy in copies:
        copy.start()
    for copy in copies:
        copy.wait()


def per_device(
    fwd_now,
    fwd_prev,
    adj_now,
    adj_prev,
    speed_sq,
    face_lists,
    send_low,
    send_high,
    send_radial,
    owner_dev,
    param_slot,
):
    operator, spread, factor, edge = constants()
    elements = fwd_now.shape[1]
    groups = lax.axis_size("group")
    layers = lax.axis_size("depth")
    devices = groups * layers
    capacity = elements // devices + elements // (2 * devices) + 2
    room = -(-capacity // 8) * 8
    vmem = pl.BlockSpec(memory_space=pltpu.VMEM)
    hbm = pl.BlockSpec(memory_space=pltpu.HBM)
    dma = pltpu.SemaphoreType.DMA
    final, grad = pl.pallas_call(
        functools.partial(kernel, (groups, layers, elements, capacity, room), edge),
        out_shape=(
            jax.ShapeDtypeStruct((2, NODES, elements), F32),
            jax.ShapeDtypeStruct((P_DEV, NODES), F32),
        ),
        in_specs=[hbm] * 14,
        out_specs=(vmem, vmem),
        scratch_shapes=[
            pltpu.VMEM((2, ROWS, elements), F32),
            pltpu.VMEM((4, NODES, elements), F32),
            pltpu.VMEM((2, ROWS, elements), F32),
            pltpu.VMEM((2, ROWS, elements), F32),
            pltpu.VMEM((3 * ROWS, elements), F32),
            pltpu.VMEM((ROWS, elements), F32),
            pltpu.VMEM((1, elements), F32),
            pltpu.VMEM((6, elements), jnp.int32),
            pltpu.VMEM((1, elements), jnp.int32),
            pltpu.VMEM((1, elements), jnp.int32),
            pltpu.VMEM(operator.shape, BF16),
            pltpu.VMEM(spread.shape, BF16),
            pltpu.VMEM(factor.shape, F32),
            pltpu.VMEM((6, elements, elements), BF16),
            pltpu.VMEM((4, elements, elements), BF16),
            pltpu.VMEM((1, send_high.shape[0]), jnp.int32),
            pltpu.VMEM((1, send_low.shape[0]), jnp.int32),
            pltpu.VMEM((1, send_radial.shape[0]), jnp.int32),
            pltpu.VMEM((3, STEPS, 2, 25, elements), F32),
            pltpu.VMEM((3, STEPS, 2, 25, elements), F32),
            pltpu.VMEM((devices, room, ROWS), F32),
            pltpu.VMEM((devices, room, ROWS), F32),
            dma((11,)),
            dma((3,)),
            dma((3,)),
            dma((3, STEPS, 2)),
            dma((3, STEPS, 2)),
            dma((devices,)),
            dma((devices,)),
        ],
        compiler_params=pltpu.CompilerParams(
            collective_id=0, has_side_effects=True, vmem_limit_bytes=64 * 2**20 - 2**19
        ),
    )(
        fwd_now,
        fwd_prev,
        adj_now,
        adj_prev,
        speed_sq[None, :],
        face_lists,
        send_low[None, :],
        send_high[None, :],
        send_radial[None, :],
        owner_dev.reshape(1, elements),
        param_slot[None, :],
        jnp.asarray(operator),
        jnp.asarray(spread),
        jnp.asarray(factor),
    )
    return pl.pallas_call(
        deliver,
        out_shape=(
            jax.ShapeDtypeStruct((NODES, elements), F32),
            jax.ShapeDtypeStruct((NODES, elements), F32),
            jax.ShapeDtypeStruct((P_DEV, NODES), F32),
        ),
        in_specs=[hbm] * 2,
        out_specs=(hbm, hbm, hbm),
        scratch_shapes=[dma((3,))],
    )(final, grad)


def solution(mesh):
    return jax.shard_map(
        per_device,
        mesh=mesh,
        in_specs=(
            P(None, ("group", "depth")),
            P(None, ("group", "depth")),
            P(None, ("group", "depth")),
            P(None, ("group", "depth")),
            P(("group", "depth")),
            P(None, ("group", "depth")),
            P(("group", "depth")),
            P(("group", "depth")),
            P(("group", "depth")),
            P(("group", "depth"), None),
            P(("group", "depth")),
        ),
        out_specs=(
            P(None, ("group", "depth")),
            P(None, ("group", "depth")),
            P(("group", "depth"), None),
        ),
        check_vma=False,
    )
```

time: 43.3 us -> 46.3 us (1.069)
  Pallas kernels: 31.9 us -> 45.5 us
  local copies, waits for them, and re-layouts: 10.4 us -> 0 us
    pallas_call x0 -> x1, Pallas kernels: none -> 11.1 us  [per_device(): pl.pallas_call(deliver, out_shape=(jax.ShapeDtypeStruct((NODES, elements)...]
    unnamed x22 -> x0, local copies, waits for them, and re-layouts: 8.25 us -> none
    pallas_call x1, Pallas kernels: 31.9 us -> 34.4 us  [per_device(): pl.pallas_call(functools.partial(kernel, (groups, layers, elements, capac...]
    concatenate x1 -> x0, local copies, waits for them, and re-layouts: 1.42 us -> none  [per_device(): jnp.concatenate([face_lists, row(send_low), row(send_high), row(send_radi...]
    pad x1 -> x0, local copies, waits for them, and re-layouts: 0.7 us -> none  [row(): jnp.pad(values, (0, elements - values.shape[0]), constant_values=-1)]
where the time goes in v2:
time: 46.3 us; the launch traced here: 46.1 us
  Pallas kernels  45.5 us (98%)
  between operations  0.64 us (1%)
    pallas_call x1, Pallas kernels, per_device(): pl.pallas_call(functools.partial(kernel, (groups, layers, elements, capac...  34.4 us
    pallas_call x1, Pallas kernels, per_device(): pl.pallas_call(deliver, out_shape=(jax.ShapeDtypeStruct((NODES, elements)...  11.1 us

profile of v2, /device:TPU:0, one launch (start us, length us, event | category | flops | bytes accessed | tf_op | source)
XLA Modules:
  0.0 46.1 jit_solution(13987589319813058868)
XLA Ops:
  0.6 34.4 %shard_map.157 = (f32[2,125,256]{2,1,0:T(8,128)}, f32[128,125]{1,0:T(8,128)}) custom-call(f32[125,256]{1,0:T(8,128)} %fwd_now.1, f32[125,256]{1,0:T(8,128)} %fwd_prev.1, f32[125,256]{1,0:T(8,128)} %adj_now.1, f32[125,256]{1,0:T(8,128)} %adj_prev.1, f32[1,256]{1,0:T(1,128)} %bitcast.6, s32[6,256]{1,0:T(8,128)} %lists_in.1, s32[1,256]{1,0:T(1,128)} %bitcast.7, ...), custom_call_target="tpu_custom_call" | custom-call | tf_op jit(solution)/shard_map/pallas_call | solution.py:426
  35.1 11.1 %shard_map.158 = (f32[125,256]{1,0:T(8,128)}, f32[125,256]{1,0:T(8,128)}, f32[128,125]{1,0:T(8,128)}) custom-call(f32[2,125,256]{2,1,0:T(8,128)} %get-tuple-element.5.final, f32[128,125]{1,0:T(8,128)} %get-tuple-element.6.grad), custom_call_target="tpu_custom_call" | custom-call | tf_op jit(solution)/shard_map/pallas_call | solution.py:484

commit v3 on v2

--- a/solution.py
+++ b/solution.py
@@ -488,7 +488,7 @@
             jax.ShapeDtypeStruct((NODES, elements), F32),
             jax.ShapeDtypeStruct((P_DEV, NODES), F32),
         ),
-        in_specs=[hbm] * 2,
+        in_specs=[vmem] * 2,
         out_specs=(hbm, hbm, hbm),
         scratch_shapes=[dma((3,))],
     )(final, grad)

time: 46.3 us -> 36.9 us (0.80)
  Pallas kernels: 45.5 us -> 36.1 us
    pallas_call x1, Pallas kernels: 11.1 us -> 1.69 us  [per_device(): pl.pallas_call(deliver, out_shape=(jax.ShapeDtypeStruct((NODES, elements)...]
where the time goes in v3:
time: 36.9 us; the launch traced here: 36.8 us
  Pallas kernels  36.1 us (98%)
  between operations  0.64 us (2%)
    pallas_call x1, Pallas kernels, per_device(): pl.pallas_call(functools.partial(kernel, (groups, layers, elements, capac...  34.4 us
    pallas_call x1, Pallas kernels, per_device(): pl.pallas_call(deliver, out_shape=(jax.ShapeDtypeStruct((NODES, elements)...  1.69 us

profile of v3, /device:TPU:0, one launch (start us, length us, event | category | flops | bytes accessed | tf_op | source)
XLA Modules:
  0.0 36.8 jit_solution(13505317449405795085)
XLA Ops:
  0.6 34.4 %shard_map.157 = (f32[2,125,256]{2,1,0:T(8,128)}, f32[128,125]{1,0:T(8,128)}) custom-call(f32[125,256]{1,0:T(8,128)} %fwd_now.1, f32[125,256]{1,0:T(8,128)} %fwd_prev.1, f32[125,256]{1,0:T(8,128)} %adj_now.1, f32[125,256]{1,0:T(8,128)} %adj_prev.1, f32[1,256]{1,0:T(1,128)} %bitcast.6, s32[6,256]{1,0:T(8,128)} %lists_in.1, s32[1,256]{1,0:T(1,128)} %bitcast.7, ...), custom_call_target="tpu_custom_call" | custom-call | tf_op jit(solution)/shard_map/pallas_call | solution.py:426
  35.1 1.7 %shard_map.158 = (f32[125,256]{1,0:T(8,128)}, f32[125,256]{1,0:T(8,128)}, f32[128,125]{1,0:T(8,128)}) custom-call(f32[2,125,256]{2,1,0:T(8,128)} %get-tuple-element.5.final, f32[128,125]{1,0:T(8,128)} %get-tuple-element.6.grad), custom_call_target="tpu_custom_call" | custom-call | tf_op jit(solution)/shard_map/pallas_call | solution.py:484
